TPU v7x, 128 devices: a whole 4x4x4 slice. The times are simulated.
128 devices in a mesh: row: 8 (over x, core), col: 16 (over y, z).
Axes of the slice: x: 4, y: 4, z: 4, core: 2. Of those that a mesh axis runs over, the one named last changes fastest.
Arguments:
- amplitudes: float32 [8, 4, 8, 16, 128, 128], P(None, None, None, 'col', 'row'), may hold values from -6 to 6
- coupling: float32 [8, 6, 128, 8, 16, 128], P(None, None, 'col', None, 'row'), may hold values from -0.0625 to 0.0625
- incoming_residual: float32 [8, 4, 8, 6, 128, 128], P('row', None, None, None, 'col'), may hold values from -6 to 6
- occupied_count: int32 [8], replicated, may hold values from 8 to 16, as said below
- virtual_count: int32 [8], replicated, may hold values from 64 to 128, as said below
Outputs:
- residual_out: float32 [8, 4, 8, 6, 128, 128], P('row', None, None, None, 'col')
Inputs may be any that keep to these rules, and one draw needn't show every extreme that they name: `occupied_count`: some irrep has exactly 16 and some exactly 8 occupied orbitals. `virtual_count`: some irrep has exactly 128 and some exactly 64 virtual orbitals.
All inputs are finite; a program needn't handle non-finite values.
Results may differ from a plain program's by a relative error of at most 0.00005.
Values sent between devices are 32-bit elements; how exact they have to be, the bound alone decides.
No kernel may reach another device: no remote copies, remote signals or barrier semaphores. Data moves between devices by JAX's collectives and lax.ppermute only.
A program may use at most 256 MiB of HBM per device.

v0:
```python
import jax
import jax.numpy as jnp
from jax import lax
from jax.sharding import PartitionSpec as P


def keep_table(counts, offset, length):
    positions = offset + jnp.arange(length, dtype=jnp.int32)
    return (positions[None, :] < counts[:, None]).astype(jnp.float32)


def shards(amplitudes, coupling, incoming_residual, occupied_count, virtual_count):
    row_index = lax.axis_index("row")
    col_index = lax.axis_index("col")
    occ_local = amplitudes.shape[3]
    vir_local = amplitudes.shape[4]
    vir_full = amplitudes.shape[5]
    keep_k = keep_table(occupied_count, col_index * occ_local, occ_local)
    keep_c = keep_table(virtual_count, row_index * vir_local, vir_local)
    keep_a = keep_table(virtual_count, 0, vir_full)
    masked_amps = (
        amplitudes
        * keep_a[:, None, None, None, None, :]
        * keep_k[None, None, :, :, None, None]
        * keep_c[None, None, :, None, :, None]
    )
    cycle_amps = lax.all_to_all(
        lax.all_to_all(masked_amps, "row", split_axis=0, concat_axis=4, tiled=True),
        "col",
        split_axis=4,
        concat_axis=3,
        tiled=True,
    )
    coupling_vir = coupling.shape[2]
    coupling_occ = coupling.shape[4]
    keep_bw = keep_table(virtual_count, col_index * coupling_vir, coupling_vir)
    keep_kw = keep_table(occupied_count, row_index * coupling_occ, coupling_occ)
    keep_cw = keep_table(virtual_count, 0, coupling.shape[5])
    masked_coupling = (
        coupling
        * keep_bw[:, None, :, None, None, None]
        * keep_kw[None, None, None, :, :, None]
        * keep_cw[None, None, None, :, None, :]
    )
    coupling_full = lax.all_gather(masked_coupling, "row", axis=4, tiled=True)
    cycle_term = jnp.einsum(
        "xiykca,gjbykc->xigjba",
        lax.all_gather(cycle_amps, "col", axis=4, tiled=True),
        coupling_full,
        precision=lax.Precision.HIGHEST,
        preferred_element_type=jnp.float32,
    )
    return incoming_residual + cycle_term


def solution(mesh):
    return jax.shard_map(
        shards,
        mesh=mesh,
        in_specs=(
            P(None, None, None, "col", "row", None),
            P(None, None, "col", None, "row", None),
            P("row", None, None, None, "col", None),
            P(),
            P(),
        ),
        out_specs=P("row", None, None, None, "col", None),
        check_vma=False,
    )
```

profile of v0, /device:TPU:0, one launch (start us, length us, event | category | flops | bytes accessed | tf_op | source)
XLA Modules:
  0.0 413.1 jit_solution(11258469092386710622)
XLA Ops:
  6.5 0.0 all-gather.3.cloned.1.call-start
  6.5 0.7 fusion.17
  7.3 0.7 compare_convert_fusion.1
  8.0 0.7 compare_convert_fusion.3
  8.7 5.1 %fusion.4 = f32[8,6,8,8,2,128]{5,2,3,4,1,0:T(8,128)} fusion(f32[8,6,8,8,2,128]{5,4,3,2,1,0:T(2,128)} %param.6, f32[8,128]{1,0:T(8,128)S(1)} %fusion.17, f32[8,2]{0,1:T(2,128)S(1)} %compare_convert_fusion.3, f32[8,8]{1,0:T(8,128)S(1)} %compare_convert_fusion.1), kind=kLoop, calls=%fused_computation.5 | loop fusion | flops 2359296 | bytes 6295872 | tf_op jit(solution)/shard_map/mul | solution.py:40
  13.8 0.0 copy-start.2
  13.8 0.0 copy-start.1
  13.8 0.0 copy-start
  13.8 0.0 all-gather.3.cloned.1.call-update
  13.8 0.0 all-gather.5.cloned.1.call-start
  13.9 0.6 copy-done.2
  14.4 0.0 copy-done.1
  14.5 0.1 compare_convert_fusion
  14.5 0.9 copy-done
  15.4 0.4 fusion.6
  15.8 46.0 %all_to_all.30 = f32[8,4,8,1,16,128]{5,4,2,1,3,0:T(8,128)S(1)} all-to-all(f32[8,4,8,1,16,128]{5,4,2,1,3,0:T(8,128)S(1)} %fusion.6), channel_id=1, replica_groups=mesh['row'=8,'col'=16] {'row'}, dimensions={0} | all-to-all | bytes 4194304 | tf_op jit(solution)/shard_map/all_to_all | solution.py:28
  61.8 0.2 copy.16
  62.0 1.2 copy.17
  63.2 36.4 %all_to_all.31 = f32[1,4,8,1,128,128]{5,2,1,3,0,4:T(8,128)S(1)} all-to-all(f32[1,4,8,1,128,128]{5,2,1,3,0,4:T(8,128)S(1)} %copy.17), channel_id=1, replica_groups=mesh['row'=8,'col'=16] {'col'}, dimensions={4} | all-to-all | bytes 4194304 | tf_op jit(solution)/shard_map/all_to_all | solution.py:27
  99.6 0.0 copy-start.3
  99.6 2.6 copy.19
  102.2 0.0 all-gather.5.cloned.1.call-update
  102.2 48.3 %all-gather.3.cloned.1.call-done = f32[8,6,8,8,16,128]{5,2,3,4,1,0:T(8,128)} async-done(((f32[8,6,8,8,2,128]{5,2,3,4,1,0:T(8,128)}), f32[8,6,8,8,16,128]{5,2,3,4,1,0:T(8,128)}) %all-gather.3.cloned.1.call-update) | async-done | bytes 25165840 | tf_op jit(solution)/shard_map/all_gather | solution.py:45
  150.6 209.2 %all-gather.5.cloned.1.call-done = f32[1,4,8,16,128,128]{5,4,2,3,1,0:T(8,128)} async-done(((f32[1,4,8,16,8,128]{5,4,2,3,1,0:T(8,128)}), f32[1,4,8,16,128,128]{5,4,2,3,1,0:T(8,128)}) %all-gather.5.cloned.1.call-update) | async-done | bytes 33554448 | tf_op jit(solution)/shard_map/all_gather | solution.py:48
  359.8 0.0 copy-done.3
  359.8 45.6 %fusion.12 = f32[1,4,8,6,8,128]{5,4,1,3,2,0:T(8,128)S(1)} fusion(f32[1,4,8,16,128,128]{5,4,2,3,1,0:T(8,128)} %all-gather.5.cloned.1.call-done, f32[8,6,8,8,16,128]{5,2,3,4,1,0:T(8,128)} %all-gather.3.cloned.1.call-done, f32[1,4,8,6,8,128]{5,4,3,2,1,0:T(8,128)S(1)} %copy-done.3), kind=kOutput, calls=%fused_computation.10 | convolution fusion | flops 38654902272 | bytes 60293120 | tf_op jit(solution)/shard_map/xiykca,gjbykc->xigjba/dot_general | solution.py:46
  405.4 0.9 copy.21
  (4 shorter events, 0.0 us)
Async XLA Ops:
  6.5 144.0 %all-gather.3.cloned.1.call-start = ((), (), s32[]{:S(2)}) async-start(), calls=%async_computation.2 | async-start | bytes 28311552 | tf_op jit(solution)/shard_map/all_gather | solution.py:45
  13.8 0.7 copy-start.2
  13.8 0.7 copy-start.1
  13.8 1.6 copy-start
  13.8 346.0 %all-gather.5.cloned.1.call-start = ((), (), s32[]{:S(2)}) async-start(), calls=%async_computation.3 | async-start | bytes 35651584 | tf_op jit(solution)/shard_map/all_gather | solution.py:48
  99.6 260.2 %copy-start.3 = (f32[1,4,8,6,8,128]{5,4,3,2,1,0:T(8,128)S(1)}, f32[1,4,8,6,8,128]{5,4,3,2,1,0:T(8,128)}, u32[]{:S(2)}) copy-start(f32[1,4,8,6,8,128]{5,4,3,2,1,0:T(8,128)} %param.7) | copy-start | bytes 2359300
Sparse Core Ops, SparseCore 0:
  13.9 136.5 all-gather.2
  152.7 207.0 all-gather.4
where the time goes:
time: 413 us
  waiting for transfers between devices  258 us (62%)
  blocking collectives  82.3 us (20%)
  matrix products  45.6 us (11%)
  between operations  13.5 us (3%)
  other arithmetic  7.7 us (2%)
  local copies, waits for them, and re-layouts  6.43 us (2%)
    all_gather x1, waiting for transfers between devices, shards(): lax.all_gather(cycle_amps, 'col', axis=4, tiled=True)  209 us
    all_gather x1, waiting for transfers between devices, shards(): coupling_full = lax.all_gather(masked_coupling, 'row', axis=4, tiled=True)  48.3 us
    all_to_all x1, blocking collectives, shards(): lax.all_to_all(masked_amps, 'row', split_axis=0, concat_axis=4, tiled=True)  46 us
    dot_general x1, matrix products, shards(): jnp.einsum('xiykca,gjbykc->xigjba', lax.all_gather(cycle_amps, 'col', axi...  45.6 us
    all_to_all x1, blocking collectives, shards(): lax.all_to_all(lax.all_to_all(masked_amps, 'row', split_axis=0, concat_ax...  36.4 us
  transfers between devices with their start and end apart: 2, of which 2 were waited for; matrix products, arithmetic and copies ran while one was open for 1% of the time, Pallas kernels for 0%

commit v1 on v0

v1 whole, which is shorter than its diff:
```python
import functools

import jax
import jax.numpy as jnp
from jax import lax
from jax.experimental import pallas as pl
from jax.experimental.pallas import tpu as pltpu
from jax.sharding import Mesh
from jax.sharding import PartitionSpec as P

NX, NC, NY, NZ = 4, 2, 4, 4
F32 = jnp.float32
BF16 = jnp.bfloat16


def split(x):
    hi = x.astype(BF16)
    lo = (x - hi.astype(F32)).astype(BF16)
    return hi, lo


ROWS_B = 96


def pack_b_kernel(info, b_ref, o_ref, acc, *, width):
    e = jnp.bitwise_xor(info[0], pl.program_id(1))
    acc[...] = jnp.zeros_like(acc)
    row = lax.broadcasted_iota(jnp.int32, (128, 256), 0)
    col = lax.broadcasted_iota(jnp.int32, (128, 256), 1)
    for y in range(8):
        off = info[1 + y]
        count = info[9 + y]
        tile = off // 128
        x = b_ref[pl.ds(2 * y + e, ROWS_B, stride=16), :]
        hi, lo = split(x)
        place = ((col == row + (off - tile * 128)) & (row < count)).astype(F32).astype(BF16)
        moved = jnp.dot(hi, place, preferred_element_type=F32)
        moved += jnp.dot(lo, place, preferred_element_type=F32)
        at = pl.ds(pl.multiple_of(tile * 128, 128), 256)
        acc[:, at] = acc[:, at] + moved
    o_ref[0] = acc[:, :width]


def pack_b(info, b2, width):
    rows = b2.shape[0] // 16
    return pl.pallas_call(
        functools.partial(pack_b_kernel, width=width),
        grid_spec=pltpu.PrefetchScalarGridSpec(
            num_scalar_prefetch=1,
            grid=(rows // ROWS_B, 2),
            in_specs=[pl.BlockSpec((ROWS_B * 16, 128), lambda r, u, info: (r, 0))],
            out_specs=pl.BlockSpec((1, ROWS_B, width), lambda r, u, info: (u, r, 0)),
            scratch_shapes=[pltpu.VMEM((ROWS_B, width + 256), F32)],
        ),
        out_shape=jax.ShapeDtypeStruct((2, rows, width), F32),
        compiler_params=pltpu.CompilerParams(vmem_limit_bytes=32 * 2**20),
        cost_estimate=pl.CostEstimate(
            flops=2 * 2 * 2 * rows * 1024 * 256, bytes_accessed=4 * rows * (2048 + 2 * width), transcendentals=0
        ),
        name="pack_coupling",
    )(info, b2)


def pack_a_kernel(tgt_ref, a0, a1, a2, a3, o_ref, hi_s, lo_s):
    step = pl.program_id(0)

    @pl.when(step == 0)
    def _():
        for s, ref in enumerate((a0, a1, a2, a3)):
            for cr in range(2):
                for i in range(4):
                    hi, lo = split(ref[cr, i])
                    at = (s * 2 + cr) * 128
                    hi_s[at : at + 128, i * 128 : (i + 1) * 128] = hi
                    lo_s[at : at + 128, i * 128 : (i + 1) * 128] = lo

    rows = lax.broadcasted_iota(jnp.int32, (128, 1024), 0) + step * 128
    pick = (rows == tgt_ref[...]).astype(F32).astype(BF16)
    out = jnp.dot(pick, hi_s[...], preferred_element_type=F32)
    out += jnp.dot(pick, lo_s[...], preferred_element_type=F32)
    o_ref[...] = out


def pack_a(tgt, parts, width):
    full = pl.BlockSpec((2, 4, 128, 128), lambda p: (0, 0, 0, 0))
    return pl.pallas_call(
        pack_a_kernel,
        grid=(width // 128,),
        in_specs=[pl.BlockSpec((1, 1024), lambda p: (0, 0))] + [full] * 4,
        out_specs=pl.BlockSpec((128, 512), lambda p: (p, 0)),
        scratch_shapes=[pltpu.VMEM((1024, 512), BF16), pltpu.VMEM((1024, 512), BF16)],
        out_shape=jax.ShapeDtypeStruct((width, 512), F32),
        compiler_params=pltpu.CompilerParams(vmem_limit_bytes=32 * 2**20),
        cost_estimate=pl.CostEstimate(
            flops=2 * 2 * width * 1024 * 512, bytes_accessed=4 * (2**19 + width * 512), transcendentals=0
        ),
        name="pack_amplitudes",
    )(tgt, *parts)


def shift_x(value, by):
    return lax.ppermute(value, "x", [(p, (p + by) % NX) for p in range(NX)])


def swap_core(value):
    return lax.ppermute(value, "c", [(0, 1), (1, 0)])


def to_k_owner(value, u):
    pairs = []
    for c in range(NC):
        for z in range(NZ):
            pairs.append((c * NZ + z, (z // 2) * NZ + 2 * c + ((z % 2) ^ u)))
    return lax.ppermute(value, ("c", "z"), pairs)


def to_home(value, u, w):
    pairs = []
    for c in range(NC):
        for z in range(NZ):
            pairs.append((c * NZ + z, ((z // 2) ^ w) * NZ + 2 * c + ((z % 2) ^ u)))
    return lax.ppermute(value, ("c", "z"), pairs)


def dot3(b, a):
    return lax.dot_general(
        b, a, (((1,), (0,)), ((), ())), precision=lax.Precision.HIGH, preferred_element_type=F32
    )


def body(amplitudes, coupling, incoming_residual, occupied_count, virtual_count, *, width):
    xi, ci, yi, zi = (lax.axis_index(n) for n in ("x", "c", "y", "z"))
    offsets = jnp.cumsum(virtual_count) - virtual_count
    info = jnp.concatenate([jnp.stack([zi % 2]), offsets, virtual_count]).astype(jnp.int32)

    amps = amplitudes.reshape(4, 2, 4, 128, 128)
    own = lax.dynamic_index_in_dim(amps, ci, 1, keepdims=False)
    got = swap_core(lax.dynamic_index_in_dim(amps, 1 - ci, 1, keepdims=False))
    both = jnp.stack([own, got])
    parts = []
    for s in range(4):
        msg = lax.dynamic_index_in_dim(both, (xi + s) % 4, 1, keepdims=False)
        parts.append(msg if s == 0 else shift_x(msg, s))

    k = yi * 4 + zi
    src_x = (xi - jnp.arange(4, dtype=jnp.int32)) % 4
    src_c = jnp.stack([ci, 1 - ci])
    chunk = 2 * src_x[:, None] + src_c[None, :]
    c_at = 16 * chunk[:, :, None, None] + jnp.arange(16, dtype=jnp.int32)
    keep = (c_at < virtual_count[:, None]) & (k < occupied_count)[:, None]
    tgt = jnp.where(keep, offsets[:, None] + c_at, -1).reshape(1, 1024).astype(jnp.int32)

    packed_b = pack_b(info, coupling.reshape(-1, 128), width)
    blocks = [to_k_owner(packed_b[u], u) for u in range(2)]

    packed_a = pack_a(tgt, parts, width)
    a_own = lax.all_gather(packed_a, "y", axis=0, tiled=False)
    a_oth = swap_core(a_own)

    def terms(b, source):
        return [dot3(b, lax.dynamic_index_in_dim(a, source, 0, keepdims=False)) for a in (a_own, a_oth)]

    h = zi // 2
    total = []
    for u in range(2):
        b = blocks[u]
        half = b.shape[0] // 2
        left, right = shift_x(b, 1), shift_x(b, -1)
        far_top, far_low = shift_x(left[:half], 1), shift_x(right[half:], -1)
        far = jnp.concatenate([far_top, far_low])
        sums = None
        for piece, dx in ((b, 0), (left, -1), (right, 1), (far, 2)):
            new = terms(piece, (xi + dx) % 4)
            sums = new if sums is None else [p + q for p, q in zip(sums, new)]
        for w in range(2):
            pick_own = ci == jnp.bitwise_xor(h, w)
            total.append(to_home(jnp.where(pick_own, sums[0], sums[1]), u, w))

    cycle = (total[0] + total[1]) + (total[2] + total[3])
    x_at = 2 * xi + ci
    b_at = 8 * (4 * yi + zi) + jnp.arange(8, dtype=jnp.int32)
    keep_b = (b_at[None, :] < virtual_count[:, None])[None, :, None, :, None]
    keep_a = jnp.arange(128, dtype=jnp.int32) < virtual_count[x_at]
    cycle = cycle.reshape(8, 6, 8, 4, 128).transpose(3, 0, 1, 2, 4)
    cycle = jnp.where(keep_b & keep_a, cycle, 0.0)
    return incoming_residual + cycle[None]


def solution(mesh):
    fine = Mesh(mesh.devices.reshape(NX, NC, NY, NZ), ("x", "c", "y", "z"))
    return jax.shard_map(
        functools.partial(body, width=1024),
        mesh=fine,
        in_specs=(
            P(None, None, None, ("y", "z"), ("x", "c"), None),
            P(None, None, ("y", "z"), None, ("x", "c"), None),
            P(("x", "c"), None, None, None, ("y", "z"), None),
            P(),
            P(),
        ),
        out_specs=P(("x", "c"), None, None, None, ("y", "z"), None),
        check_vma=False,
    )
```

time: 413 us -> 364 us (0.88)
  blocking collectives: 82.3 us -> 0 us
  starting transfers between devices: 0.04 us -> 25.6 us
  local copies, waits for them, and re-layouts: 6.43 us -> 19.7 us
  waiting for transfers between devices: 258 us -> 247 us
  Pallas kernels: 0 us -> 9.04 us
    all_gather x2 -> x1, waiting for transfers between devices: 258 us -> 84.5 us  [body(): a_own = lax.all_gather(packed_a, 'y', axis=0, tiled=False)]
    ppermute x0 -> x19, waiting for transfers between devices: none -> 162 us  [the longest x11 110 us: shift_x(): return lax.ppermute(value, 'x', [(p, (p + by) % NX) for p in range(NX)])]
    all_to_all x2 -> x0, blocking collectives: 82.3 us -> none  [the longest x1 46 us: shards(): lax.all_to_all(masked_amps, 'row', split_axis=0, concat_axis=4, tiled=True)]
    ppermute x0 -> x19, starting transfers between devices: none -> 25.6 us  [the longest x11 14.8 us: shift_x(): return lax.ppermute(value, 'x', [(p, (p + by) % NX) for p in range(NX)])]
    unnamed x8 -> x46, local copies, waits for them, and re-layouts: 1.46 us -> 10.5 us
    pallas_call x0 -> x2, Pallas kernels: none -> 9.04 us  [the longest x1 5.06 us: pack_b(): pl.pallas_call(functools.partial(pack_b_kernel, width=width), grid_spec=p...]
    mul x2, other arithmetic: 5.44 us -> 0.08 us  [the longest x1 0.07 us: body(): c_at = 16 * chunk[:, :, None, None] + jnp.arange(16, dtype=jnp.int32)]
    dot_general x1 -> x16, matrix products: 45.6 us -> 42.5 us  [dot3(): lax.dot_general(b, a, (((1,), (0,)), ((), ())), precision=lax.Precision.H...]
  transfers between devices with their start and end apart: 2 -> 20, of which waited for: 2 -> 10; matrix products, arithmetic and copies ran while one was open for 1% -> 11% of each run, Pallas kernels for 0% -> 1%
where the time goes in v1:
time: 364 us; the launch traced here: 363 us
  waiting for transfers between devices  247 us (68%)
  matrix products  42.5 us (12%)
  starting transfers between devices  25.6 us (7%)
  local copies, waits for them, and re-layouts  19.7 us (5%)
  between operations  13.9 us (4%)
  Pallas kernels  9.04 us (2%)
  other arithmetic  5.53 us (2%)
    ppermute x11, waiting for transfers between devices, shift_x(): return lax.ppermute(value, 'x', [(p, (p + by) % NX) for p in range(NX)])  110 us
    all_gather x1, waiting for transfers between devices, body(): a_own = lax.all_gather(packed_a, 'y', axis=0, tiled=False)  84.5 us
    dot_general x16, matrix products, dot3(): lax.dot_general(b, a, (((1,), (0,)), ((), ())), precision=lax.Precision.H...  42.5 us
    ppermute x2, waiting for transfers between devices, to_k_owner(): return lax.ppermute(value, ('c', 'z'), pairs)  31.4 us
    ppermute x4, waiting for transfers between devices, to_home(): return lax.ppermute(value, ('c', 'z'), pairs)  18.9 us
    ppermute x11, starting transfers between devices, shift_x(): return lax.ppermute(value, 'x', [(p, (p + by) % NX) for p in range(NX)])  14.8 us
    unnamed x46, local copies, waits for them, and re-layouts  10.5 us
    ppermute x4, starting transfers between devices, to_home(): return lax.ppermute(value, ('c', 'z'), pairs)  8.27 us
  transfers between devices with their start and end apart: 20, of which 10 were waited for; matrix products, arithmetic and copies ran while one was open for 11% of the time, Pallas kernels for 1%

profile of v1, /device:TPU:0, one launch (start us, length us, event | category | flops | bytes accessed | tf_op | source)
XLA Modules:
  0.0 363.0 jit_solution(12571385586372880054)
XLA Ops:
  6.5 1.7 dynamic-slice_bitcast_fusion
  8.7 2.2 collective-permute-done.1
  11.0 1.2 fusion.85
  12.2 1.6 collective-permute-start.2
  13.8 2.7 collective-permute-start.3
  16.5 1.4 collective-permute-start.4
  18.2 9.4 %collective-permute-done.2.a1 = f32[2,4,128,128]{3,2,1,0:T(8,128)S(1)} collective-permute-done((f32[2,4,128,128]{3,2,1,0:T(8,128)}, f32[2,4,128,128]{3,2,1,0:T(8,128)S(1)}, u32[]{:S(2)}, u32[]{:S(2)}) %collective-permute-start.2) | collective-permute-done | bytes 524320 | tf_op jit(solution)/shard_map/ppermute | solution.py:102
  27.6 0.8 copy-done.3
  28.4 11.5 %collective-permute-done.3.a2 = f32[2,4,128,128]{3,2,1,0:T(8,128)S(1)} collective-permute-done((f32[2,4,128,128]{3,2,1,0:T(8,128)}, f32[2,4,128,128]{3,2,1,0:T(8,128)S(1)}, u32[]{:S(2)}, u32[]{:S(2)}) %collective-permute-start.3) | collective-permute-done | bytes 524320 | tf_op jit(solution)/shard_map/ppermute | solution.py:102
  39.9 0.8 copy-done.5
  40.7 0.8 copy-done.7
  41.5 1.0 copy-done.2
  42.6 1.0 copy-done.4
  43.6 1.0 copy-done.6
  44.7 1.0 copy-done.8
  45.7 4.0 %pack_amplitudes.1 = f32[1024,512]{1,0:T(8,128)S(1)} custom-call(s32[1,1024]{1,0:T(1,128)S(1)} %select_n.146.tgt_ref, f32[2,4,128,128]{3,2,1,0:T(8,128)S(1)} %copy-done.2, f32[2,4,128,128]{3,2,1,0:T(8,128)S(1)} %copy-done.4, f32[2,4,128,128]{3,2,1,0:T(8,128)S(1)} %copy-done.6, f32[2,4,128,128]{3,2,1,0:T(8,128)S(1)} %copy-done.8), custom_call_target="tpu_custom_call" | custom-call | flops 2147483648 | bytes 4194304 | tf_op jit(solution)/shard_map/pack_amplitudes/pallas_call | solution.py:86
  49.7 1.3 copy-done.1
  51.1 84.5 %all-gather.3.cloned.1.call-done = f32[4096,512]{1,0:T(8,128)} async-done(((f32[1024,512]{1,0:T(8,128)}), f32[4096,512]{1,0:T(8,128)}) %all-gather.3.cloned.1.call-update) | async-done | bytes 8388624 | tf_op jit(solution)/shard_map/all_gather | solution.py:157
  135.6 5.1 %pack_coupling.1 = f32[2,384,1024]{2,1,0:T(8,128)S(1)} custom-call(s32[17]{0:T(128)S(1)} %pad_add_fusion.info, f32[6144,128]{1,0:T(8,128)S(1)} %bitcast.118), custom_call_target="tpu_custom_call" | custom-call | flops 805306368 | bytes 6291456 | tf_op jit(solution)/shard_map/pack_coupling/pallas_call | solution.py:46
  141.1 1.6 collective-permute-start.12
  142.7 0.7 collective-permute-start
  143.5 31.4 %collective-permute-done.12 = f32[384,1024]{1,0:T(8,128)S(1)} collective-permute-done((f32[384,1024]{1,0:T(8,128)S(1)}, f32[384,1024]{1,0:T(8,128)S(1)}, u32[]{:S(2)}, u32[]{:S(2)}) %collective-permute-start.12) | collective-permute-done | bytes 1572896 | tf_op jit(solution)/shard_map/ppermute | solution.py:114
  174.9 1.5 collective-permute-start.13
  176.4 1.5 collective-permute-start.5
  177.8 1.8 collective-permute-start.14
  179.6 0.6 collective-permute-start.6
  180.2 30.5 %collective-permute-done.13 = f32[384,1024]{1,0:T(8,128)S(1)} collective-permute-done((f32[384,1024]{1,0:T(8,128)S(1)}, f32[384,1024]{1,0:T(8,128)S(1)}, u32[]{:S(2)}, u32[]{:S(2)}) %collective-permute-start.13) | collective-permute-done | bytes 1572896 | tf_op jit(solution)/shard_map/ppermute | solution.py:102
  210.7 1.0 slice.28
  212.0 32.4 %collective-permute-done.5 = f32[384,1024]{1,0:T(8,128)S(1)} collective-permute-done((f32[384,1024]{1,0:T(8,128)S(1)}, f32[384,1024]{1,0:T(8,128)S(1)}, u32[]{:S(2)}, u32[]{:S(2)}) %collective-permute-start.5) | collective-permute-done | bytes 1572896 | tf_op jit(solution)/shard_map/ppermute | solution.py:102
  244.4 1.0 slice.25
  245.7 1.1 slice.29
  246.8 3.0 collective-permute-start.16
  249.7 0.9 slice.26
  251.1 10.3 %collective-permute-done.15 = f32[192,1024]{1,0:T(8,128)} collective-permute-done((f32[192,1024]{1,0:T(8,128)}, f32[192,1024]{1,0:T(8,128)}, u32[]{:S(2)}, u32[]{:S(2)}) %collective-permute-start.15) | collective-permute-done | bytes 786464 | tf_op jit(solution)/shard_map/ppermute | solution.py:102
  261.4 1.3 constant_dynamic-update-slice_fusion.3
  262.7 15.5 %collective-permute-done.7 = f32[192,1024]{1,0:T(8,128)} collective-permute-done((f32[192,1024]{1,0:T(8,128)}, f32[192,1024]{1,0:T(8,128)}, u32[]{:S(2)}, u32[]{:S(2)}) %collective-permute-start.7) | collective-permute-done | bytes 786464 | tf_op jit(solution)/shard_map/ppermute | solution.py:102
  278.2 1.2 constant_dynamic-update-slice_fusion.1
  279.4 1.2 constant_dynamic-update-slice_fusion.2
  280.6 1.2 constant_dynamic-update-slice_fusion
  281.8 3.2 fusion.16
  285.1 3.2 fusion.18
  288.4 1.6 fusion.20
  290.0 1.6 fusion.28
  291.6 1.6 fusion.22
  293.2 1.6 fusion.30
  294.8 3.1 fusion
  297.9 3.1 fusion.4
  301.0 3.4 fusion.12
  304.5 3.1 fusion.81
  307.6 2.9 broadcast_select_fusion
  310.5 3.6 collective-permute-start.17
  314.1 2.1 collective-permute-start.18
  316.2 3.1 fusion.2
  319.3 3.1 fusion.6
  322.4 3.1 fusion.14
  325.5 3.1 fusion.72
  328.6 1.7 broadcast_select_fusion.1
  330.3 0.8 collective-permute-start.10
  331.1 1.7 collective-permute-start.11
  332.9 0.7 dynamic_slice.56
  333.5 0.6 iota_compare_fusion
  334.3 18.9 %collective-permute-done.18 = f32[384,512]{1,0:T(8,128)} collective-permute-done((f32[384,512]{1,0:T(8,128)}, f32[384,512]{1,0:T(8,128)}, u32[]{:S(2)}, u32[]{:S(2)}) %collective-permute-start.18) | collective-permute-done | bytes 786464 | tf_op jit(solution)/shard_map/ppermute | solution.py:122
  353.2 2.0 add_add_fusion
  355.2 1.0 bitcast_add_fusion
  (68 shorter events, 2.3 us)
Async XLA Ops:
  6.5 129.0 %all-gather.3.cloned.1.call-start = ((), (), s32[]{:S(2)}) async-start(), calls=%async_computation | async-start | bytes 10485760 | tf_op jit(solution)/shard_map/all_gather | solution.py:157
  6.5 1.9 copy-start.18
  8.2 2.7 collective-permute-start.1
  11.0 7.0 %copy-start.19 = (s32[8]{0:T(128)S(1)}, s32[8]{0:T(128)}, u32[]{:S(2)}) copy-start(s32[8]{0:T(128)} %param.8) | copy-start | bytes 100
  12.2 15.4 %collective-permute-start.2 = (f32[2,4,128,128]{3,2,1,0:T(8,128)}, f32[2,4,128,128]{3,2,1,0:T(8,128)S(1)}, u32[]{:S(2)}, u32[]{:S(2)}) collective-permute-start(f32[2,4,128,128]{3,2,1,0:T(8,128)} %get-tuple-element.9), channel_id=1, source_target_pairs={{0,32},{32,64},{64,96},{96,0},{1,33},{33,65},{65,97},{97,1},{2,34}... | collective-permute-start | bytes 1572872 | tf_op jit(solution)/shard_map/ppermute | solution.py:102
  13.8 26.1 %collective-permute-start.3 = (f32[2,4,128,128]{3,2,1,0:T(8,128)}, f32[2,4,128,128]{3,2,1,0:T(8,128)S(1)}, u32[]{:S(2)}, u32[]{:S(2)}) collective-permute-start(f32[2,4,128,128]{3,2,1,0:T(8,128)} %get-tuple-element.10), channel_id=1, source_target_pairs={{0,64},{32,96},{64,0},{96,32},{1,65},{33,97},{65,1},{97,33},{2,66}... | collective-permute-start | bytes 1572872 | tf_op jit(solution)/shard_map/ppermute | solution.py:102
  16.5 24.2 %collective-permute-start.4 = (f32[2,4,128,128]{3,2,1,0:T(8,128)S(1)}, f32[2,4,128,128]{3,2,1,0:T(8,128)S(1)}, u32[]{:S(2)}, u32[]{:S(2)}) collective-permute-start(f32[2,4,128,128]{3,2,1,0:T(8,128)S(1)} %get-tuple-element.7), channel_id=1, source_target_pairs={{0,96},{32,0},{64,32},{96,64},{1,97},{33,1},{65,33},{97,65},{2,98}... | collective-permute-start | bytes 1572872 | tf_op jit(solution)/shard_map/ppermute | solution.py:102
  27.6 0.8 copy-start.3
  39.9 0.8 copy-start.5
  40.7 0.8 copy-start.7
  41.5 1.0 copy-start.2
  42.6 1.0 copy-start.4
  43.6 1.0 copy-start.6
  44.7 1.0 copy-start.8
  45.7 89.9 %copy-start = (f32[8,6,8,8,2,128]{5,4,3,2,1,0:T(2,128)S(1)}, f32[8,6,8,8,2,128]{5,4,3,2,1,0:T(2,128)}, u32[]{:S(2)}) copy-start(f32[8,6,8,8,2,128]{5,4,3,2,1,0:T(2,128)} %param.6) | copy-start | bytes 9437188
  49.7 1.3 copy-start.1
  135.5 159.3 %collective-permute-start.9 = (f32[4,1024,512]{2,1,0:T(8,128)}, f32[4,1024,512]{2,1,0:T(8,128)}, u32[]{:S(2)}, u32[]{:S(2)}) collective-permute-start(f32[4,1024,512]{2,1,0:T(8,128)} %bitcast.119), channel_id=1, source_target_pairs={{0,16},{16,0},{1,17},{17,1},{2,18},{18,2},{3,19},{19,3},{4,20},{20... | collective-permute-start | bytes 25165832 | tf_op jit(solution)/shard_map/ppermute | solution.py:106
  141.1 33.8 %collective-permute-start.12 = (f32[384,1024]{1,0:T(8,128)S(1)}, f32[384,1024]{1,0:T(8,128)S(1)}, u32[]{:S(2)}, u32[]{:S(2)}) collective-permute-start(f32[384,1024]{1,0:T(8,128)S(1)} %get-tuple-element.6), channel_id=1, source_target_pairs={{0,1},{1,0},{2,17},{3,16},{16,3},{17,2},{18,19},{19,18},{4,5},{5,4... | collective-permute-start | bytes 4718600 | tf_op jit(solution)/shard_map/ppermute | solution.py:114
  142.7 33.6 %collective-permute-start = (f32[384,1024]{1,0:T(8,128)S(1)}, f32[384,1024]{1,0:T(8,128)S(1)}, u32[]{:S(2)}, u32[]{:S(2)}) collective-permute-start(f32[384,1024]{1,0:T(8,128)S(1)} %get-tuple-element.5), channel_id=1, source_target_pairs={{0,0},{1,1},{2,16},{3,17},{16,2},{17,3},{18,18},{19,19},{4,4},{5,5... | collective-permute-start | bytes 4718600 | tf_op jit(solution)/shard_map/ppermute | solution.py:114
  174.9 75.8 %copy-start.15 = (f32[384,1024]{1,0:T(8,128)}, f32[384,1024]{1,0:T(8,128)S(1)}, u32[]{:S(2)}) copy-start(f32[384,1024]{1,0:T(8,128)S(1)} %collective-permute-done.12) | copy-start | bytes 4718596
  174.9 35.8 %collective-permute-start.13 = (f32[384,1024]{1,0:T(8,128)S(1)}, f32[384,1024]{1,0:T(8,128)S(1)}, u32[]{:S(2)}, u32[]{:S(2)}) collective-permute-start(f32[384,1024]{1,0:T(8,128)S(1)} %collective-permute-done.12), channel_id=1, source_target_pairs={{0,32},{32,64},{64,96},{96,0},{1,33},{33,65},{65,97},{97,1},{2,34}... | collective-permute-start | bytes 4718600 | tf_op jit(solution)/shard_map/ppermute | solution.py:102
  176.4 70.4 %copy-start.13 = (f32[384,1024]{1,0:T(8,128)}, f32[384,1024]{1,0:T(8,128)S(1)}, u32[]{:S(2)}) copy-start(f32[384,1024]{1,0:T(8,128)S(1)} %collective-permute-done) | copy-start | bytes 4718596
  176.4 68.1 %collective-permute-start.5 = (f32[384,1024]{1,0:T(8,128)S(1)}, f32[384,1024]{1,0:T(8,128)S(1)}, u32[]{:S(2)}, u32[]{:S(2)}) collective-permute-start(f32[384,1024]{1,0:T(8,128)S(1)} %collective-permute-done), channel_id=1, source_target_pairs={{0,32},{32,64},{64,96},{96,0},{1,33},{33,65},{65,97},{97,1},{2,34}... | collective-permute-start | bytes 4718600 | tf_op jit(solution)/shard_map/ppermute | solution.py:102
  177.8 67.9 %collective-permute-start.14 = (f32[384,1024]{1,0:T(8,128)S(1)}, f32[384,1024]{1,0:T(8,128)S(1)}, u32[]{:S(2)}, u32[]{:S(2)}) collective-permute-start(f32[384,1024]{1,0:T(8,128)S(1)} %collective-permute-done.12), channel_id=1, source_target_pairs={{0,96},{32,0},{64,32},{96,64},{1,97},{33,1},{65,33},{97,65},{2,98}... | collective-permute-start | bytes 4718600 | tf_op jit(solution)/shard_map/ppermute | solution.py:102
  179.6 70.1 %collective-permute-start.6 = (f32[384,1024]{1,0:T(8,128)S(1)}, f32[384,1024]{1,0:T(8,128)S(1)}, u32[]{:S(2)}, u32[]{:S(2)}) collective-permute-start(f32[384,1024]{1,0:T(8,128)S(1)} %collective-permute-done), channel_id=1, source_target_pairs={{0,96},{32,0},{64,32},{96,64},{1,97},{33,1},{65,33},{97,65},{2,98}... | collective-permute-start | bytes 4718600 | tf_op jit(solution)/shard_map/ppermute | solution.py:102
  210.7 36.0 %copy-start.9 = (f32[384,1024]{1,0:T(8,128)}, f32[384,1024]{1,0:T(8,128)S(1)}, u32[]{:S(2)}) copy-start(f32[384,1024]{1,0:T(8,128)S(1)} %collective-permute-done.13) | copy-start | bytes 4718596
  211.7 49.7 %collective-permute-start.15 = (f32[192,1024]{1,0:T(8,128)}, f32[192,1024]{1,0:T(8,128)}, u32[]{:S(2)}, u32[]{:S(2)}) collective-permute-start(f32[192,1024]{1,0:T(8,128)} %slice.28), channel_id=1, source_target_pairs={{0,32},{32,64},{64,96},{96,0},{1,33},{33,65},{65,97},{97,1},{2,34}... | collective-permute-start | bytes 2359304 | tf_op jit(solution)/shard_map/ppermute | solution.py:102
  245.4 32.8 %collective-permute-start.7 = (f32[192,1024]{1,0:T(8,128)}, f32[192,1024]{1,0:T(8,128)}, u32[]{:S(2)}, u32[]{:S(2)}) collective-permute-start(f32[192,1024]{1,0:T(8,128)} %slice.25), channel_id=1, source_target_pairs={{0,32},{32,64},{64,96},{96,0},{1,33},{33,65},{65,97},{97,1},{2,34}... | collective-permute-start | bytes 2359304 | tf_op jit(solution)/shard_map/ppermute | solution.py:102
  245.7 4.1 %copy-start.11 = (f32[384,1024]{1,0:T(8,128)}, f32[384,1024]{1,0:T(8,128)S(1)}, u32[]{:S(2)}) copy-start(f32[384,1024]{1,0:T(8,128)S(1)} %collective-permute-done.14) | copy-start | bytes 4718596
  246.8 32.7 %collective-permute-start.16 = (f32[192,1024]{1,0:T(8,128)}, f32[192,1024]{1,0:T(8,128)}, u32[]{:S(2)}, u32[]{:S(2)}) collective-permute-start(f32[192,1024]{1,0:T(8,128)} %slice.29), channel_id=1, source_target_pairs={{0,96},{32,0},{64,32},{96,64},{1,97},{33,1},{65,33},{97,65},{2,98}... | collective-permute-start | bytes 2359304 | tf_op jit(solution)/shard_map/ppermute | solution.py:102
  250.7 29.9 %collective-permute-start.8 = (f32[192,1024]{1,0:T(8,128)}, f32[192,1024]{1,0:T(8,128)}, u32[]{:S(2)}, u32[]{:S(2)}) collective-permute-start(f32[192,1024]{1,0:T(8,128)} %slice.26), channel_id=1, source_target_pairs={{0,96},{32,0},{64,32},{96,64},{1,97},{33,1},{65,33},{97,65},{2,98}... | collective-permute-start | bytes 2359304 | tf_op jit(solution)/shard_map/ppermute | solution.py:102
  261.4 26.9 %slice-start = ((s8[8388608]{0:T(1024)(128)(4,1)}), s8[4194304]{0:T(1024)(128)(4,1)S(1)}, s32[]{:S(2)}) async-start(s8[8388608]{0:T(1024)(128)(4,1)} %bitcast.122), calls=%async_computation.1 | async-start | bytes 8388608
  281.8 6.5 %slice-start.1 = ((s8[8388608]{0:T(1024)(128)(4,1)}), s8[4194304]{0:T(1024)(128)(4,1)S(1)}, s32[]{:S(2)}) async-start(s8[8388608]{0:T(1024)(128)(4,1)} %bitcast.122), calls=%async_computation.2 | async-start | bytes 8388608
  285.1 3.2 copy-start.12
  288.3 1.6 copy-start.16
  291.6 1.6 copy-start.14
  301.0 3.5 copy-start.10
  310.5 23.8 %collective-permute-start.17 = (f32[384,512]{1,0:T(8,128)}, f32[384,512]{1,0:T(8,128)}, u32[]{:S(2)}, u32[]{:S(2)}) collective-permute-start(f32[384,512]{1,0:T(8,128)} %get-tuple-element.16), channel_id=1, source_target_pairs={{0,1},{1,0},{2,17},{3,16},{16,3},{17,2},{18,19},{19,18},{4,5},{5,4... | collective-permute-start | bytes 2359304 | tf_op jit(solution)/shard_map/ppermute | solution.py:122
  314.1 39.1 %collective-permute-start.18 = (f32[384,512]{1,0:T(8,128)}, f32[384,512]{1,0:T(8,128)}, u32[]{:S(2)}, u32[]{:S(2)}) collective-permute-start(f32[384,512]{1,0:T(8,128)} %get-tuple-element.15), channel_id=1, source_target_pairs={{0,17},{1,16},{2,1},{3,0},{16,19},{17,18},{18,3},{19,2},{4,21},{5,... | collective-permute-start | bytes 2359304 | tf_op jit(solution)/shard_map/ppermute | solution.py:122
  330.3 24.9 %copy-start.17 = (f32[1,4,8,6,8,128]{5,4,3,2,1,0:T(8,128)S(1)}, f32[1,4,8,6,8,128]{5,4,3,2,1,0:T(8,128)}, u32[]{:S(2)}) copy-start(f32[1,4,8,6,8,128]{5,4,3,2,1,0:T(8,128)} %param.7) | copy-start | bytes 2359300
  330.3 22.9 %collective-permute-start.10 = (f32[384,512]{1,0:T(8,128)S(1)}, f32[384,512]{1,0:T(8,128)S(1)}, u32[]{:S(2)}, u32[]{:S(2)}) collective-permute-start(f32[384,512]{1,0:T(8,128)S(1)} %get-tuple-element.14), channel_id=1, source_target_pairs={{0,0},{1,1},{2,16},{3,17},{16,2},{17,3},{18,18},{19,19},{4,4},{5,5... | collective-permute-start | bytes 2359304 | tf_op jit(solution)/shard_map/ppermute | solution.py:122
  331.1 22.1 %collective-permute-start.11 = (f32[384,512]{1,0:T(8,128)S(1)}, f32[384,512]{1,0:T(8,128)}, u32[]{:S(2)}, u32[]{:S(2)}) collective-permute-start(f32[384,512]{1,0:T(8,128)S(1)} %get-tuple-element.13), channel_id=1, source_target_pairs={{0,16},{1,17},{2,0},{3,1},{16,18},{17,19},{18,2},{19,3},{4,20},{5,... | collective-permute-start | bytes 2359304 | tf_op jit(solution)/shard_map/ppermute | solution.py:122
Sparse Core Ops, SparseCore 0:
  51.2 84.3 all-gather.2
